TPU v7x, 32 devices: a whole 2x2x4 slice. The times are simulated.
32 devices in a mesh: group: 2 (over x), attn: 8 (over z, y), expert: 2 (over core).
Axes of the slice: x: 2, y: 2, z: 4, core: 2. Of those that a mesh axis runs over, the one named last changes fastest.
Arguments:
- queries: bfloat16 [256, 6144], P(('group', 'attn'), 'expert'), parts along dimension 0, may hold values from -6 to 6
- new_kv: bfloat16 [256, 2, 1024], P(('group', 'attn'), None, 'expert'), parts along dimension 0, may hold values from -6 to 6
- cache_kv: bfloat16 [256, 2, 16, 1024], P(('group', 'attn'), None, None, 'expert'), parts along dimension 0, may hold values from -6 to 6
- lengths: int32 [256], P(('group', 'attn')), parts along dimension 0, may hold values from 1 to 16, as said below
- residual: bfloat16 [256, 6144], P(('group', 'attn'), 'expert'), parts along dimension 0, may hold values from -12 to 12
- norm_gain: bfloat16 [6144], replicated, may hold values from 0.099609375 to 1.8984375
- expert_ids: int32 [256, 2], P(('group', 'attn')), parts along dimension 0, may hold values from 0 to 3, all different within a row; in each aligned block of 16 rows (0 to 15, 16 to 31, ...) at most 12 rows name the same one
- route_weights: bfloat16 [256, 2], P(('group', 'attn')), parts along dimension 0, may hold values from 0.19921875 to 1
- w_up: bfloat16 [6144, 32768], P(None, ('attn', 'expert')), may hold values from -0.078125 to 0.078125
- w_down: bfloat16 [32768, 6144], P(('attn', 'expert')), may hold values from -0.0625 to 0.0625
Outputs:
- layer_out: bfloat16 [256, 6144], P(('group', 'attn'), 'expert'), parts along dimension 0
There are 2 independent parts, one for each index of `group`. A program takes and returns all parts, laid end to end along the dimension named above; an argument that names none is the same for every part. Nothing has to cross between parts.
Inputs may be any that keep to these rules, and one draw needn't show every extreme that they name: Request t holds valid cache entries at positions 0 to lengths[t] - 1; in every draw some request holds all 16. `expert_ids`: each token names 2 different experts. Among the 16 tokens of one device's rows no expert is named more than 12 times, and in every draw some expert is named exactly 12 times in some device's rows.
All inputs are finite; a program needn't handle non-finite values.
Results may differ from a plain program's by a relative error of at most 0.012.
Values may be sent and summed in bfloat16 or wider, within the bound.
A program may use at most 128 MiB of HBM per device.

v0:
```python
import jax
import jax.numpy as jnp
from jax import lax
from jax.sharding import PartitionSpec as P

HEAD_DIM = 128
EXPERTS = 4
CAP = 12


EPSILON = 1e-05
NEG_FILL = -1e30


def attend(queries, new_kv, cache_kv, lengths):
    tok_rows = queries.shape[0]
    kv_heads = new_kv.shape[-1] // HEAD_DIM
    group_size = queries.shape[1] // (kv_heads * HEAD_DIM)
    cache_len = cache_kv.shape[2]
    scaling = HEAD_DIM ** (-0.5)
    query_vec = queries.astype(jnp.float32).reshape(tok_rows, kv_heads, group_size, HEAD_DIM)
    key_cache = cache_kv[:, 0].astype(jnp.float32).reshape(tok_rows, cache_len, kv_heads, HEAD_DIM)
    value_cache = (
        cache_kv[:, 1].astype(jnp.float32).reshape(tok_rows, cache_len, kv_heads, HEAD_DIM)
    )
    new_key = new_kv[:, 0].astype(jnp.float32).reshape(tok_rows, kv_heads, HEAD_DIM)
    new_value = new_kv[:, 1].astype(jnp.float32).reshape(tok_rows, kv_heads, HEAD_DIM)
    visible = (jnp.arange(cache_len)[None, :] < lengths[:, None])[:, None, None, :]
    old_scores = jnp.einsum("tkgd,tskd->tkgs", query_vec, key_cache) * scaling
    old_scores = jnp.where(visible, old_scores, NEG_FILL)
    new_scores = jnp.einsum("tkgd,tkd->tkg", query_vec, new_key) * scaling
    row_max = jnp.maximum(jnp.max(old_scores, axis=-1), new_scores)
    old_probs = jnp.where(visible, jnp.exp(old_scores - row_max[..., None]), 0.0)
    new_probs = jnp.exp(new_scores - row_max)
    totals = jnp.sum(old_probs, axis=-1) + new_probs
    old_weight = lax.optimization_barrier(
        (old_probs / totals[..., None]).astype(jnp.bfloat16)
    ).astype(jnp.float32)
    new_weight = lax.optimization_barrier((new_probs / totals).astype(jnp.bfloat16)).astype(
        jnp.float32
    )
    attended = (
        jnp.einsum("tkgs,tskd->tkgd", old_weight, value_cache)
        + new_weight[..., None] * new_value[:, :, None, :]
    )
    return attended.reshape(tok_rows, -1).astype(jnp.bfloat16)


def normalize(stream_rows, norm_gain):
    widened = stream_rows.astype(jnp.float32)
    mean_square = jnp.mean(widened * widened, axis=-1, keepdims=True)
    return (widened * lax.rsqrt(mean_square + EPSILON) * norm_gain.astype(jnp.float32)).astype(
        jnp.bfloat16
    )


def local(
    queries, new_kv, cache_kv, lengths, residual, norm_gain, expert_ids, route_weights, w_up, w_down
):
    attended = attend(queries, new_kv, cache_kv, lengths)
    stream = (residual.astype(jnp.float32) + attended.astype(jnp.float32)).astype(jnp.bfloat16)
    tok_rows = stream.shape[0]
    top_count = expert_ids.shape[1]
    members = lax.axis_size("attn") // EXPERTS
    flat_expert = expert_ids.reshape(-1)
    one_hot = (flat_expert[:, None] == jnp.arange(EXPERTS)[None, :]).astype(jnp.int32)
    earlier = jnp.cumsum(one_hot, axis=0) - one_hot
    slot_index = flat_expert * CAP + jnp.sum(earlier * one_hot, axis=1)
    placing = jnp.arange(EXPERTS * CAP)[:, None] == slot_index[None, :]
    by_token = jnp.sum(
        placing.reshape(EXPERTS * CAP, tok_rows, top_count).astype(jnp.int32), axis=2
    ).astype(jnp.bfloat16)
    slot_rows = jnp.dot(by_token, stream, preferred_element_type=jnp.float32).astype(jnp.bfloat16)
    send_rows = jnp.repeat(slot_rows.reshape(EXPERTS, CAP, -1), members, axis=0)
    arrived = lax.all_to_all(send_rows, "attn", split_axis=0, concat_axis=0, tiled=True)
    arrived = lax.all_gather(arrived, "expert", axis=2, tiled=True)
    normed = normalize(arrived.reshape(-1, arrived.shape[2]), norm_gain)
    up_proj = jnp.dot(normed, w_up, preferred_element_type=jnp.float32)
    hidden = jax.nn.silu(up_proj).astype(jnp.bfloat16)
    partial_value = jnp.dot(hidden, w_down, preferred_element_type=jnp.float32)
    partial_value = partial_value.reshape(arrived.shape[0], arrived.shape[1], -1)
    shares = lax.psum_scatter(partial_value, "expert", scatter_dimension=2, tiled=True)
    returned = lax.all_to_all(shares, "attn", split_axis=0, concat_axis=0, tiled=True)
    per_expert = jnp.sum(returned.reshape(EXPERTS, members, CAP, -1), axis=1).reshape(
        EXPERTS * CAP, -1
    )
    picked = jnp.take(per_expert, slot_index, axis=0).reshape(tok_rows, top_count, -1)
    mixture = jnp.sum(picked * route_weights.astype(jnp.float32)[:, :, None], axis=1)
    return (stream.astype(jnp.float32) + mixture).astype(jnp.bfloat16)


def solution(mesh):
    in_specs = (
        P(("group", "attn"), "expert"),
        P(("group", "attn"), None, "expert"),
        P(("group", "attn"), None, None, "expert"),
        P(("group", "attn")),
        P(("group", "attn"), "expert"),
        P(),
        P(("group", "attn"), None),
        P(("group", "attn"), None),
        P(None, ("attn", "expert")),
        P(("attn", "expert"), None),
    )
    out_specs = P(("group", "attn"), "expert")
    return jax.shard_map(local, mesh=mesh, in_specs=in_specs, out_specs=out_specs, check_vma=False)
```

profile of v0, /device:TPU:0, one launch (start us, length us, event | category | flops | bytes accessed | tf_op | source)
XLA Modules:
  0.0 142.3 jit_solution(5821168928334043178)
XLA Ops:
  6.5 0.7 iota_compare_fusion.2
  7.3 1.1 fusion.21
  8.3 0.0 copy-start.2
  8.3 0.0 copy-start
  8.4 0.1 reshape.147
  8.4 1.0 reshape.146
  9.5 0.8 slice_convert_fusion
  10.3 1.0 fusion.11
  11.2 0.3 fusion.22
  11.6 0.3 fusion.10
  11.9 0.2 divide_convert_fusion
  12.2 0.1 reshape.149
  12.2 0.2 fusion.5
  12.5 0.1 copy.27
  12.6 0.1 reshape.150
  12.7 0.1 fusion.14
  12.8 0.1 reduce_window_sum.11
  12.8 0.2 select_reduce_fusion
  13.0 0.1 reduce_sum.60
  13.1 0.1 copy.28
  13.2 0.1 convert_reduce_fusion
  13.3 0.3 convolution_convert_fusion
  13.6 0.1 reshape.151
  13.6 0.1 broadcast_in_dim.47
  13.7 27.3 %all_to_all.10 = bf16[8,12,3072]{2,1,0:T(8,128)(2,1)} all-to-all(bf16[8,12,3072]{2,1,0:T(8,128)(2,1)S(1)} %bitcast.24), channel_id=1, replica_groups=mesh['group'=2,'attn'=8,'expert'=2] {'attn'}, dimensions={0} | all-to-all | bytes 1179648 | tf_op jit(solution)/shard_map/all_to_all | solution.py:75
  41.1 0.0 all-gather.2.cloned.1.call-update
  41.1 0.0 reduce-scatter.2.cloned.1.call-start
  41.1 8.9 %all-gather.2.cloned.1.call-done = bf16[8,12,6144]{2,1,0:T(8,128)(2,1)} async-done(((bf16[8,12,3072]{2,1,0:T(8,128)(2,1)}), bf16[8,12,6144]{2,1,0:T(8,128)(2,1)}) %all-gather.2.cloned.1.call-update) | async-done | bytes 1179664 | tf_op jit(solution)/shard_map/all_gather | solution.py:76
  50.1 1.8 %multiply_reduce_fusion = f32[8,12]{1,0:T(8,128)S(1)} fusion(bf16[8,12,6144]{2,1,0:T(8,128)(2,1)} %all-gather.2.cloned.1.call-done), kind=kLoop, calls=%fused_computation.2 | loop fusion | flops 1769376 | bytes 1180032 | tf_op jit(solution)/shard_map/reduce_sum | solution.py:51
  51.9 0.1 rsqrt.12
  52.0 1.5 %reshape.158 = f32[96,6144]{1,0:T(8,128)S(1)} reshape(bf16[8,12,6144]{2,1,0:T(8,128)(2,1)} %all-gather.2.cloned.1.call-done) | data formatting | bytes 3538944 | tf_op jit(solution)/shard_map/convert_element_type | solution.py:50
  53.5 21.0 %fusion.6 = f32[96,6144]{1,0:T(8,128)} fusion(bf16[2048,6144]{1,0:T(8,128)(2,1)} %param.19, bf16[6144,2048]{1,0:T(8,128)(2,1)} %param.18, f32[96,6144]{1,0:T(8,128)S(1)} %reshape.158, f32[6144]{0:T(1024)S(1)} %convert_element_type.97, f32[96]{0:T(128)S(1)} %rsqrt.12), kind=kOutput, calls=%fused_computation.14 | convolution fusion | flops 4834590720 | bytes 55075200 | tf_op jit(solution)/shard_map/dot_general | solution.py:80
  74.6 3.1 %reshape.153 = f32[8,12,6144]{2,1,0:T(8,128)} reshape(f32[96,6144]{1,0:T(8,128)} %fusion.6) | data formatting | bytes 4718592 | tf_op jit(solution)/shard_map/reshape | solution.py:81
  77.6 0.0 reduce-scatter.2.cloned.1.call-update
  77.6 0.0 copy-start.3
  77.7 12.2 %reduce-scatter.2.cloned.1.call-done = f32[8,12,3072]{2,1,0:T(8,128)} async-done(((f32[8,12,6144]{2,1,0:T(8,128)}), f32[8,12,3072]{2,1,0:T(8,128)}) %reduce-scatter.2.cloned.1.call-update) | async-done | bytes 1179664 | tf_op jit(solution)/shard_map/reduce_scatter | solution.py:82
  89.9 5.7 %all-to-all-start.1 = ((f32[8,12,3072]{2,1,0:T(8,128)}), f32[8,12,3072]{2,1,0:T(8,128)S(1)}, u32[]{:S(2)}, u32[]{:S(2)}) async-start(f32[8,12,3072]{2,1,0:T(8,128)} %reduce-scatter.2.cloned.1.call-done), calls=%async_computation.2 | async-start | bytes 3145728 | tf_op jit(solution)/shard_map/all_to_all | solution.py:83
  95.6 0.1 copy.30
  95.7 0.1 mul.99
  95.8 0.1 copy.29
  95.9 0.1 copy.31
  96.0 37.1 %all-to-all-done.1 = f32[8,12,3072]{2,1,0:T(8,128)S(1)} async-done(((f32[8,12,3072]{2,1,0:T(8,128)}), f32[8,12,3072]{2,1,0:T(8,128)S(1)}, u32[]{:S(2)}, u32[]{:S(2)}) %all-to-all-start.1) | async-done | bytes 1179680 | tf_op jit(solution)/shard_map/all_to_all | solution.py:83
  133.1 0.1 bitcast_reduce_fusion
  133.2 0.1 reshape.155
  133.3 0.7 gather_fusion
  134.0 0.2 gather.7
  134.2 0.6 multiply_reduce_fusion.1
  134.8 0.7 add_convert_fusion
  (16 shorter events, 0.2 us)
Async XLA Ops:
  6.5 43.5 %all-gather.2.cloned.1.call-start = ((), (), s32[]{:S(2)}) async-start(), calls=%async_computation.3 | async-start | bytes 2359296 | tf_op jit(solution)/shard_map/all_gather | solution.py:76
  8.3 4.2 %copy-start.2 = (s32[16,2]{0,1:T(2,128)S(1)}, s32[16,2]{0,1:T(2,128)}, u32[]{:S(2)}) copy-start(s32[16,2]{0,1:T(2,128)} %param.16) | copy-start | bytes 388
  8.3 4.9 %copy-start = (bf16[16,3072]{1,0:T(8,128)(2,1)S(1)}, bf16[16,3072]{1,0:T(8,128)(2,1)}, u32[]{:S(2)}) copy-start(bf16[16,3072]{1,0:T(8,128)(2,1)} %param.14) | copy-start | bytes 294916
  13.3 27.8 %copy-start.1 = (bf16[6144]{0:T(1024)(128)(2,1)S(1)}, bf16[6144]{0:T(1024)(128)(2,1)}, u32[]{:S(2)}) copy-start(bf16[6144]{0:T(1024)(128)(2,1)} %param.15) | copy-start | bytes 36868
  41.1 48.8 %reduce-scatter.2.cloned.1.call-start = ((), (), s32[]{:S(2)}) async-start(), calls=%async_computation.4 | async-start | bytes 4718592 | tf_op jit(solution)/shard_map/reduce_scatter | solution.py:82
  77.6 18.3 %copy-start.3 = (bf16[16,2]{0,1:T(2,128)(2,1)S(1)}, bf16[16,2]{0,1:T(2,128)(2,1)}, u32[]{:S(2)}) copy-start(bf16[16,2]{0,1:T(2,128)(2,1)} %param.17) | copy-start | bytes 196
  89.9 43.2 %all-to-all-start.1 = ((f32[8,12,3072]{2,1,0:T(8,128)}), f32[8,12,3072]{2,1,0:T(8,128)S(1)}, u32[]{:S(2)}, u32[]{:S(2)}) async-start(f32[8,12,3072]{2,1,0:T(8,128)} %reduce-scatter.2.cloned.1.call-done), calls=%async_computation.2 | async-start | bytes 3145728 | tf_op jit(solution)/shard_map/all_to_all | solution.py:83
Sparse Core Ops, SparseCore 0:
  41.2 8.8 all-gather.1
  77.8 12.0 reduce-scatter.1
where the time goes:
time: 143 us; the launch traced here: 142 us
  waiting for transfers between devices  58.3 us (41%)
  blocking collectives  27.3 us (19%)
  matrix products  22.8 us (16%)
  between operations  13.6 us (10%)
  local copies, waits for them, and re-layouts  8.82 us (6%)
  starting transfers between devices  5.79 us (4%)
  other arithmetic  5.71 us (4%)
    all_to_all x1, waiting for transfers between devices, local(): lax.all_to_all(shares, 'attn', split_axis=0, concat_axis=0, tiled=True)  37.1 us
    all_to_all x1, blocking collectives, local(): lax.all_to_all(send_rows, 'attn', split_axis=0, concat_axis=0, tiled=True)  27.3 us
    dot_general x1, matrix products, local(): partial_value = jnp.dot(hidden, w_down, preferred_element_type=jnp.float32)  21 us
    reduce_scatter x1, waiting for transfers between devices, local(): lax.psum_scatter(partial_value, 'expert', scatter_dimension=2, tiled=True)  12.2 us
    all_gather x1, waiting for transfers between devices, local(): arrived = lax.all_gather(arrived, 'expert', axis=2, tiled=True)  8.9 us
    all_to_all x1, starting transfers between devices, local(): lax.all_to_all(shares, 'attn', split_axis=0, concat_axis=0, tiled=True)  5.75 us
    reshape x1, local copies, waits for them, and re-layouts, local(): partial_value.reshape(arrived.shape[0], arrived.shape[1], -1)  3.07 us
  transfers between devices with their start and end apart: 3, of which 3 were waited for; matrix products, arithmetic and copies ran while one was open for 0% of the time, Pallas kernels for 0%

commit v1 on v0

v1 whole, which is shorter than its diff:
```python
import functools

import jax
import jax.numpy as jnp
from jax import lax
from jax.experimental import pallas as pl
from jax.experimental.pallas import tpu as pltpu
from jax.sharding import PartitionSpec as P

HEAD_DIM = 128
EXPERTS = 4
EPSILON = 1e-05
NEG_FILL = -1e30
MESH = pl.DeviceIdType.MESH
CHUNKS = 4
PIECES = 8
F32 = jnp.float32
BF16 = jnp.bfloat16


def kernel(
    m, q_ref, nkv_ref, cache_ref, res_ref, gain_ref, meta_ref, wu_hbm, wd_hbm, out_ref,
    wu, wd, x, normed, hidden, core_out, core_in, keep, mem_out, mem_in, exp_out, exp_in,
    wu_sem, wd_sem, x_recv, e_send, m_send, c_send,
    co_send, co_recv, mo_send, mo_recv, eo_send, eo_recv,
):
    a = lax.axis_index("attn")
    c = lax.axis_index("expert")
    e = lax.div(a, m)
    j = lax.rem(a, m)
    core = {"attn": a, "expert": 1 - c}
    rows, half = q_ref.shape
    width = half // CHUNKS

    def expert_at(k):
        return lax.rem(e + k, EXPERTS)

    def member_at(k):
        return lax.rem(j + k, m)

    def device(ee, jj):
        return {"attn": ee * m + jj, "expert": c}

    peers = [device(expert_at(k), j) for k in range(1, EXPERTS)]
    peers += [device(e, member_at(k)) for k in range(1, m)] + [core]
    barrier = pltpu.get_barrier_semaphore()
    for peer in peers:
        pl.semaphore_signal(barrier, inc=1, device_id=peer, device_id_type=MESH)

    up_step, down_step = wu.shape[0] // PIECES, wd.shape[0] // PIECES

    def up_copy(i):
        part = pl.ds(i * up_step, up_step)
        return pltpu.make_async_copy(wu_hbm.at[part], wu.at[part], wu_sem.at[i])

    def down_copy(i):
        part = pl.ds(i * down_step, down_step)
        return pltpu.make_async_copy(wd_hbm.at[part], wd.at[part], wd_sem.at[i])

    for i in range(PIECES):
        up_copy(i).start()
    for i in range(PIECES):
        down_copy(i).start()

    kv_heads = nkv_ref.shape[1] // (2 * HEAD_DIM)
    group = half // (kv_heads * HEAD_DIM)
    cache_len = cache_ref.shape[2]
    scaling = HEAD_DIM ** (-0.5)
    shape = (group * rows, rows * cache_len)
    row_tok = lax.rem(lax.broadcasted_iota(jnp.int32, shape, 0), rows)
    col = lax.broadcasted_iota(jnp.int32, shape, 1)
    col_tok = lax.div(col, cache_len)
    col_pos = lax.rem(col, cache_len).astype(F32)
    lens = jnp.concatenate([meta_ref[:, 4:5]] * group, axis=0)
    visible = (row_tok == col_tok) & (col_pos < lens)
    for g in range(kv_heads):
        cols = pl.ds(g * HEAD_DIM, HEAD_DIM)
        heads = [pl.ds((g * group + i) * HEAD_DIM, HEAD_DIM) for i in range(group)]
        query = jnp.concatenate([q_ref[:, h] for h in heads], axis=0)
        keys = cache_ref[:, 0, :, cols].reshape(rows * cache_len, HEAD_DIM)
        values = cache_ref[:, 1, :, cols].reshape(rows * cache_len, HEAD_DIM)
        new_key = jnp.concatenate([nkv_ref[:, cols].astype(F32)] * group, axis=0)
        new_value = nkv_ref[:, pl.ds((kv_heads + g) * HEAD_DIM, HEAD_DIM)].astype(F32)
        new_value = jnp.concatenate([new_value] * group, axis=0)
        old = lax.dot_general(
            query, keys, (((1,), (1,)), ((), ())), preferred_element_type=F32
        ) * scaling
        old = jnp.where(visible, old, NEG_FILL)
        new = jnp.sum(query.astype(F32) * new_key, axis=1, keepdims=True) * scaling
        top = jnp.maximum(jnp.max(old, axis=1, keepdims=True), new)
        old_p = jnp.where(visible, jnp.exp(old - top), 0.0)
        new_p = jnp.exp(new - top)
        total = jnp.sum(old_p, axis=1, keepdims=True) + new_p
        old_w = (old_p / total).astype(BF16)
        new_w = (new_p / total).astype(BF16).astype(F32)
        attended = jnp.dot(old_w, values, preferred_element_type=F32) + new_w * new_value
        attended = attended.astype(BF16).astype(F32)
        for i, h in enumerate(heads):
            piece = attended[i * rows : (i + 1) * rows]
            x[c, j, e, :, h] = (res_ref[:, h].astype(F32) + piece).astype(BF16)

    pl.semaphore_wait(barrier, len(peers))

    def move(part, jj, ee, send, recv, peer):
        block = x.at[part, jj, ee]
        return pltpu.make_async_remote_copy(
            src_ref=block, dst_ref=block, send_sem=send, recv_sem=recv,
            device_id=peer, device_id_type=MESH,
        )

    def over_experts(k):
        return move(c, j, e, e_send.at[k], x_recv.at[0, j, e], device(expert_at(k), j))

    def over_members(k, i):
        ee = expert_at(i)
        return move(c, j, ee, m_send.at[k, i], x_recv.at[0, j, ee], device(e, member_at(k)))

    def over_cores(k, i):
        jj, ee = member_at(k), expert_at(i)
        return move(c, jj, ee, c_send.at[k, i], x_recv.at[1, jj, ee], core)

    def arrived(other, jj, ee):
        part = 1 - c if other else c
        move(part, jj, ee, e_send.at[0], x_recv.at[other, jj, ee], core).wait_recv()

    sent = []

    def start(copy):
        copy.start()
        sent.append(copy)

    for k in (2, 1, 3):
        start(over_experts(k))
    for i in (0, 1, 3, 2):
        if i:
            arrived(0, j, expert_at(i))
        for k in range(1, m):
            start(over_members(k, i))
        start(over_cores(0, i))

    order = [(0, i) for i in (0, 1, 3, 2)]
    later = [(k, i) for i in (0, 1, 3, 2) for k in range(1, m)]

    def normalize(k, i):
        jj, ee = member_at(k), expert_at(i)
        arrived(1, jj, ee)
        low = x[0, jj, ee].astype(F32)
        high = x[1, jj, ee].astype(F32)
        square = jnp.sum(low * low, axis=1, keepdims=True)
        square = square + jnp.sum(high * high, axis=1, keepdims=True)
        scale = lax.rsqrt(square / (2 * half) + EPSILON)
        normed[jj, ee, :, pl.ds(0, half)] = (
            low * scale * gain_ref[:, pl.ds(0, half)].astype(F32)
        ).astype(BF16)
        normed[jj, ee, :, pl.ds(half, half)] = (
            high * scale * gain_ref[:, pl.ds(half, half)].astype(F32)
        ).astype(BF16)

    for k, i in later:
        arrived(0, member_at(k), expert_at(i))
        start(over_cores(k, i))
        if order:
            normalize(*order.pop(0))
    for k, i in order + later:
        normalize(k, i)

    for i in range(PIECES):
        up_copy(i).wait()
    tokens = EXPERTS * m * rows
    step = 256

    @pl.loop(0, wu.shape[1] // step)
    def _(n):
        cols = pl.ds(pl.multiple_of(n * step, step), step)
        up = jnp.dot(
            normed[...].reshape(tokens, 2 * half), wu[:, cols], preferred_element_type=F32
        )
        hidden[:, cols] = (up / (1.0 + jnp.exp(-up))).astype(BF16)

    for i in range(PIECES):
        down_copy(i).wait()

    def project(part, n):
        cols = pl.ds(pl.multiple_of(part * half + n * width, 128), width)
        value = jnp.dot(hidden[...], wd[:, cols], preferred_element_type=F32)
        return value.reshape(m, EXPERTS, rows, width)

    def remote(src, dst, send, recv, peer):
        return pltpu.make_async_remote_copy(
            src_ref=src, dst_ref=dst, send_sem=send, recv_sem=recv,
            device_id=peer, device_id_type=MESH,
        )

    def core_copy(n):
        return remote(core_out.at[n], core_in.at[n], co_send.at[n], co_recv.at[n], core)

    def member_copy(n, k):
        jj = member_at(k)
        return remote(
            mem_out.at[n, jj], mem_in.at[n, j], mo_send.at[n, k], mo_recv.at[n, j], device(e, jj)
        )

    def member_arrived(n, k):
        jj = member_at(k)
        remote(
            mem_out.at[n, jj], mem_in.at[n, jj], mo_send.at[n, k], mo_recv.at[n, jj], device(e, jj)
        ).wait_recv()
        return mem_in[n, jj].astype(F32)

    def expert_copy(n, k):
        ee = expert_at(k)
        return remote(
            exp_out.at[n, ee], exp_in.at[n, e], eo_send.at[n, k], eo_recv.at[n, e], device(ee, j)
        )

    def expert_arrived(n, k):
        ee = expert_at(k)
        remote(
            exp_out.at[n, ee], exp_in.at[n, ee], eo_send.at[n, k], eo_recv.at[n, ee], device(ee, j)
        ).wait_recv()
        return exp_in[n, ee].astype(F32)

    def compute(n):
        core_out[n] = project(1 - c, n).astype(BF16)
        start(core_copy(n))
        keep[n % 2] = project(c, n)

    def sum_cores(n):
        core_copy(n).wait_recv()
        mem_out[n] = (keep[n % 2] + core_in[n].astype(F32)).astype(BF16)
        for k in range(1, m):
            start(member_copy(n, k))

    def sum_members(n):
        total = mem_out[n, j].astype(F32)
        for k in range(1, m):
            total = total + member_arrived(n, k)
        exp_out[n] = total.astype(BF16)
        for k in (2, 1, 3):
            start(expert_copy(n, k))

    def weight(ee):
        ids = meta_ref[:, 0:2]
        return jnp.sum(
            jnp.where(ids == ee.astype(F32), meta_ref[:, 2:4], 0.0), axis=1, keepdims=True
        )

    def finish(n):
        cols = pl.ds(n * width, width)
        total = weight(e) * exp_out[n, e].astype(F32)
        for k in range(1, EXPERTS):
            total = total + weight(expert_at(k)) * expert_arrived(n, k)
        out_ref[:, cols] = (x[c, j, e, :, cols].astype(F32) + total).astype(BF16)

    for n in range(CHUNKS + 2):
        if n < CHUNKS:
            compute(n)
            sum_cores(n)
        if 1 <= n <= CHUNKS:
            sum_members(n - 1)
        if n >= CHUNKS:
            for i in (range(CHUNKS - 1) if n == CHUNKS else [CHUNKS - 1]):
                finish(i)
    for copy in sent:
        copy.wait_send()


def local(
    queries, new_kv, cache_kv, lengths, residual, norm_gain, expert_ids, route_weights, w_up, w_down
):
    rows, half = queries.shape
    attn = lax.axis_size("attn")
    m = attn // EXPERTS
    width = half // CHUNKS
    meta = jnp.concatenate(
        [expert_ids.astype(F32), route_weights.astype(F32), lengths.astype(F32)[:, None]], axis=1
    )
    vmem = pl.BlockSpec(memory_space=pltpu.VMEM)
    hbm = pl.BlockSpec(memory_space=pl.ANY)
    dma = pltpu.SemaphoreType.DMA
    tokens = attn * rows
    return pl.pallas_call(
        functools.partial(kernel, m),
        out_shape=jax.ShapeDtypeStruct((rows, half), BF16),
        in_specs=[vmem] * 6 + [hbm] * 2,
        out_specs=vmem,
        scratch_shapes=[
            pltpu.VMEM(w_up.shape, BF16),
            pltpu.VMEM(w_down.shape, BF16),
            pltpu.VMEM((2, m, EXPERTS, rows, half), BF16),
            pltpu.VMEM((m, EXPERTS, rows, 2 * half), BF16),
            pltpu.VMEM((tokens, w_up.shape[1]), BF16),
            pltpu.VMEM((CHUNKS, m, EXPERTS, rows, width), BF16),
            pltpu.VMEM((CHUNKS, m, EXPERTS, rows, width), BF16),
            pltpu.VMEM((2, m, EXPERTS, rows, width), F32),
            pltpu.VMEM((CHUNKS, m, EXPERTS, rows, width), BF16),
            pltpu.VMEM((CHUNKS, m, EXPERTS, rows, width), BF16),
            pltpu.VMEM((CHUNKS, EXPERTS, rows, width), BF16),
            pltpu.VMEM((CHUNKS, EXPERTS, rows, width), BF16),
            dma((PIECES,)),
            dma((PIECES,)),
            dma((2, m, EXPERTS)),
            dma((EXPERTS,)),
            dma((m, EXPERTS)),
            dma((m, EXPERTS)),
            dma((CHUNKS,)),
            dma((CHUNKS,)),
            dma((CHUNKS, m)),
            dma((CHUNKS, m)),
            dma((CHUNKS, EXPERTS)),
            dma((CHUNKS, EXPERTS)),

        ],
        compiler_params=pltpu.CompilerParams(
            collective_id=0, has_side_effects=True, vmem_limit_bytes=62 * 2**20
        ),
    )(
        queries, new_kv.reshape(rows, -1), cache_kv, residual, norm_gain.reshape(1, -1), meta,
        w_up, w_down,
    )


def solution(mesh):
    in_specs = (
        P(("group", "attn"), "expert"),
        P(("group", "attn"), None, "expert"),
        P(("group", "attn"), None, None, "expert"),
        P(("group", "attn")),
        P(("group", "attn"), "expert"),
        P(),
        P(("group", "attn"), None),
        P(("group", "attn"), None),
        P(None, ("attn", "expert")),
        P(("attn", "expert"), None),
    )
    out_specs = P(("group", "attn"), "expert")
    return jax.shard_map(local, mesh=mesh, in_specs=in_specs, out_specs=out_specs, check_vma=False)
```

time: 143 us -> 56.6 us (0.40)
  waiting for transfers between devices: 58.3 us -> 0 us
  Pallas kernels: 0 us -> 49.1 us
  blocking collectives: 27.3 us -> 0 us
  matrix products: 22.8 us -> 0 us
  between operations: 13.6 us -> 0.01 us
  starting transfers between devices: 5.79 us -> 0 us
  other arithmetic: 5.71 us -> 2.01 us
  local copies, waits for them, and re-layouts: 8.82 us -> 5.15 us
    pallas_call x0 -> x1, Pallas kernels: none -> 49.1 us  [local(): pl.pallas_call(functools.partial(kernel, m), out_shape=jax.ShapeDtypeStru...]
    all_to_all x1 -> x0, waiting for transfers between devices: 37.1 us -> none  [local(): lax.all_to_all(shares, 'attn', split_axis=0, concat_axis=0, tiled=True)]
    all_to_all x1 -> x0, blocking collectives: 27.3 us -> none  [local(): lax.all_to_all(send_rows, 'attn', split_axis=0, concat_axis=0, tiled=True)]
    dot_general x5 -> x0, matrix products: 22.8 us -> none  [the longest x1 21 us: local(): partial_value = jnp.dot(hidden, w_down, preferred_element_type=jnp.float32)]
    reduce_scatter x1 -> x0, waiting for transfers between devices: 12.2 us -> none  [local(): lax.psum_scatter(partial_value, 'expert', scatter_dimension=2, tiled=True)]
    all_gather x1 -> x0, waiting for transfers between devices: 8.9 us -> none  [local(): arrived = lax.all_gather(arrived, 'expert', axis=2, tiled=True)]
    all_to_all x1 -> x0, starting transfers between devices: 5.75 us -> none  [local(): lax.all_to_all(shares, 'attn', split_axis=0, concat_axis=0, tiled=True)]
    reshape x7 -> x1, local copies, waits for them, and re-layouts: 4.46 us -> 1.32 us  [local(): norm_gain.reshape(1, -1)]
  transfers between devices with their start and end apart: 3 -> 0, of which waited for: 3 -> 0; matrix products, arithmetic and copies ran while one was open for 0% -> 0% of each run, Pallas kernels for 0% -> 0%
where the time goes in v1:
time: 56.6 us; the launch traced here: 56.3 us
  Pallas kernels  49.1 us (87%)
  local copies, waits for them, and re-layouts  5.15 us (9%)
  other arithmetic  2.01 us (4%)
    pallas_call x1, Pallas kernels, local(): pl.pallas_call(functools.partial(kernel, m), out_shape=jax.ShapeDtypeStru...  49.1 us
    unnamed x2, local copies, waits for them, and re-layouts  2.92 us
    reshape x1, local copies, waits for them, and re-layouts, local(): norm_gain.reshape(1, -1)  1.32 us

profile of v1, /device:TPU:0, one launch (start us, length us, event | category | flops | bytes accessed | tf_op | source)
XLA Modules:
  0.0 56.3 jit_solution(347256492305971625)
XLA Ops:
  0.0 0.7 %convert_bitcast_fusion = f32[16,1]{0,1:T(1,128)S(1)} fusion(s32[16]{0:T(128)} %param.13), kind=kLoop, calls=%fused_computation.1 | loop fusion | flops 16 | bytes 128 | tf_op jit(solution)/shard_map/broadcast_in_dim | solution.py:276
  0.7 0.7 %convert_element_type.9 = f32[16,2]{0,1:T(2,128)S(1)} convert(s32[16,2]{0,1:T(2,128)} %param.16) | non-fusion elementwise | flops 32 | bytes 256 | tf_op jit(solution)/shard_map/convert_element_type | solution.py:276
  1.3 0.1 copy.11
  1.4 0.1 copy.13
  1.5 0.7 %copy.12 = f32[16,2]{1,0:T(8,128)S(1)} copy(bf16[16,2]{0,1:T(2,128)(2,1)} %param.17) | data formatting | bytes 192 | tf_op jit(solution)/shard_map/convert_element_type | solution.py:276
  2.2 0.7 %pad_maximum_fusion.meta_ref = f32[16,5]{1,0:T(8,128)} fusion(f32[16,1]{1,0:T(8,128)S(1)} %copy.13, f32[16,2]{1,0:T(8,128)S(1)} %copy.12, f32[16,2]{1,0:T(8,128)S(1)} %copy.11), kind=kLoop, calls=%fused_computation | loop fusion | flops 160 | bytes 640 | tf_op jit(solution)/shard_map/concatenate | solution.py:275
  2.9 1.3 %reshape.7.gain_ref = bf16[1,6144]{1,0:T(2,128)(2,1)} reshape(bf16[6144]{0:T(1024)(128)(2,1)} %param.15) | data formatting | bytes 24576 | tf_op jit(solution)/shard_map/reshape | solution.py:318
  4.2 1.4 %copy.14 = bf16[2,8,2,512]{3,1,2,0:T(8,128)(2,1)} copy(bf16[2,8,2,512]{3,2,1,0:T(2,128)(2,1)} %bitcast.5) | data formatting | bytes 65536
  5.6 49.1 %shard_map.100 = bf16[16,3072]{1,0:T(8,128)(2,1)} custom-call(bf16[16,3072]{1,0:T(8,128)(2,1)} %q_ref.1, bf16[16,1024]{1,0:T(8,128)(2,1)} %bitcast.4, bf16[16,2,16,512]{3,2,1,0:T(8,128)(2,1)} %cache_ref.1, bf16[16,3072]{1,0:T(8,128)(2,1)} %res_ref.1, bf16[1,6144]{1,0:T(2,128)(2,1)} %reshape.7.gain_ref, f32[16,5]{1,0:T(8,128)} %pad_maximum_fusion.meta_ref, ...), custom_call_target="tpu_custom_call" | custom-call | tf_op jit(solution)/shard_map/pallas_call | solution.py:282
  54.7 1.5 %copy.16 = bf16[16,3072]{1,0:T(8,128)(2,1)} copy(bf16[16,3072]{1,0:T(8,128)(2,1)} %shard_map.100) | data formatting | bytes 196608

commit v2 on v1

--- a/solution.py
+++ b/solution.py
@@ -12,14 +12,14 @@
 EPSILON = 1e-05
 NEG_FILL = -1e30
 MESH = pl.DeviceIdType.MESH
-CHUNKS = 4
+CHUNKS = 2
 PIECES = 8
 F32 = jnp.float32
 BF16 = jnp.bfloat16
 
 
 def kernel(
-    m, q_ref, nkv_ref, cache_ref, res_ref, gain_ref, meta_ref, wu_hbm, wd_hbm, out_ref,
+    m, q_ref, nkv_ref, cache_ref, res_ref, gain_ref, len_ref, id_ref, route_ref, wu_hbm, wd_hbm, out_ref,
     wu, wd, x, normed, hidden, core_out, core_in, keep, mem_out, mem_in, exp_out, exp_in,
     wu_sem, wd_sem, x_recv, e_send, m_send, c_send,
     co_send, co_recv, mo_send, mo_recv, eo_send, eo_recv,
@@ -62,7 +62,7 @@
     for i in range(PIECES):
         down_copy(i).start()
 
-    kv_heads = nkv_ref.shape[1] // (2 * HEAD_DIM)
+    kv_heads = nkv_ref.shape[2] // HEAD_DIM
     group = half // (kv_heads * HEAD_DIM)
     cache_len = cache_ref.shape[2]
     scaling = HEAD_DIM ** (-0.5)
@@ -70,8 +70,8 @@
     row_tok = lax.rem(lax.broadcasted_iota(jnp.int32, shape, 0), rows)
     col = lax.broadcasted_iota(jnp.int32, shape, 1)
     col_tok = lax.div(col, cache_len)
-    col_pos = lax.rem(col, cache_len).astype(F32)
-    lens = jnp.concatenate([meta_ref[:, 4:5]] * group, axis=0)
+    col_pos = lax.rem(col, cache_len)
+    lens = jnp.concatenate([len_ref[...]] * group, axis=0)
     visible = (row_tok == col_tok) & (col_pos < lens)
     for g in range(kv_heads):
         cols = pl.ds(g * HEAD_DIM, HEAD_DIM)
@@ -79,8 +79,8 @@
         query = jnp.concatenate([q_ref[:, h] for h in heads], axis=0)
         keys = cache_ref[:, 0, :, cols].reshape(rows * cache_len, HEAD_DIM)
         values = cache_ref[:, 1, :, cols].reshape(rows * cache_len, HEAD_DIM)
-        new_key = jnp.concatenate([nkv_ref[:, cols].astype(F32)] * group, axis=0)
-        new_value = nkv_ref[:, pl.ds((kv_heads + g) * HEAD_DIM, HEAD_DIM)].astype(F32)
+        new_key = jnp.concatenate([nkv_ref[:, 0, cols].astype(F32)] * group, axis=0)
+        new_value = nkv_ref[:, 1, cols].astype(F32)
         new_value = jnp.concatenate([new_value] * group, axis=0)
         old = lax.dot_general(
             query, keys, (((1,), (1,)), ((), ())), preferred_element_type=F32
@@ -150,10 +150,10 @@
         square = square + jnp.sum(high * high, axis=1, keepdims=True)
         scale = lax.rsqrt(square / (2 * half) + EPSILON)
         normed[jj, ee, :, pl.ds(0, half)] = (
-            low * scale * gain_ref[:, pl.ds(0, half)].astype(F32)
+            low * scale * gain_ref[pl.ds(0, half)].reshape(1, half).astype(F32)
         ).astype(BF16)
         normed[jj, ee, :, pl.ds(half, half)] = (
-            high * scale * gain_ref[:, pl.ds(half, half)].astype(F32)
+            high * scale * gain_ref[pl.ds(half, half)].reshape(1, half).astype(F32)
         ).astype(BF16)
 
     for k, i in later:
@@ -240,10 +240,8 @@
             start(expert_copy(n, k))
 
     def weight(ee):
-        ids = meta_ref[:, 0:2]
-        return jnp.sum(
-            jnp.where(ids == ee.astype(F32), meta_ref[:, 2:4], 0.0), axis=1, keepdims=True
-        )
+        routed = jnp.where(id_ref[...] == ee, route_ref[...].astype(F32), 0.0)
+        return jnp.sum(routed, axis=1, keepdims=True)
 
     def finish(n):
         cols = pl.ds(n * width, width)
@@ -272,9 +270,6 @@
     attn = lax.axis_size("attn")
     m = attn // EXPERTS
     width = half // CHUNKS
-    meta = jnp.concatenate(
-        [expert_ids.astype(F32), route_weights.astype(F32), lengths.astype(F32)[:, None]], axis=1
-    )
     vmem = pl.BlockSpec(memory_space=pltpu.VMEM)
     hbm = pl.BlockSpec(memory_space=pl.ANY)
     dma = pltpu.SemaphoreType.DMA
@@ -282,7 +277,7 @@
     return pl.pallas_call(
         functools.partial(kernel, m),
         out_shape=jax.ShapeDtypeStruct((rows, half), BF16),
-        in_specs=[vmem] * 6 + [hbm] * 2,
+        in_specs=[vmem] * 8 + [hbm] * 2,
         out_specs=vmem,
         scratch_shapes=[
             pltpu.VMEM(w_up.shape, BF16),
@@ -315,7 +310,7 @@
             collective_id=0, has_side_effects=True, vmem_limit_bytes=62 * 2**20
         ),
     )(
-        queries, new_kv.reshape(rows, -1), cache_kv, residual, norm_gain.reshape(1, -1), meta,
+        queries, new_kv, cache_kv, residual, norm_gain, lengths[:, None], expert_ids, route_weights,
         w_up, w_down,
     )
 

time: 56.6 us -> 53.6 us (0.947)
  other arithmetic: 2.01 us -> 0 us
  Pallas kernels: 49.1 us -> 47.8 us
    reshape x1 -> x0, local copies, waits for them, and re-layouts: 1.32 us -> none  [local(): norm_gain.reshape(1, -1)]
    unnamed x2 -> x3, local copies, waits for them, and re-layouts: 2.92 us -> 4.22 us
    pallas_call x1, Pallas kernels: 49.1 us -> 47.8 us  [local(): pl.pallas_call(functools.partial(kernel, m), out_shape=jax.ShapeDtypeStru...]
    broadcast_in_dim x1, local copies, waits for them, and re-layouts: 0.08 us -> 1.33 us  [local(): lengths[:, None]]
    convert_element_type x2 -> x0, local copies, waits for them, and re-layouts: 0.82 us -> none  [the longest x1 0.74 us: local(): route_weights.astype(F32)]
    convert_element_type x1 -> x0, other arithmetic: 0.68 us -> none  [local(): expert_ids.astype(F32)]
    concatenate x1 -> x0, other arithmetic: 0.67 us -> none  [local(): jnp.concatenate([expert_ids.astype(F32), route_weights.astype(F32), lengt...]
    broadcast_in_dim x1 -> x0, other arithmetic: 0.66 us -> none  [local(): lengths.astype(F32)[:, None]]
where the time goes in v2:
time: 53.6 us; the launch traced here: 53.4 us
  Pallas kernels  47.8 us (89%)
  local copies, waits for them, and re-layouts  5.55 us (10%)
    pallas_call x1, Pallas kernels, local(): pl.pallas_call(functools.partial(kernel, m), out_shape=jax.ShapeDtypeStru...  47.8 us
    unnamed x3, local copies, waits for them, and re-layouts  4.22 us
    broadcast_in_dim x1, local copies, waits for them, and re-layouts, local(): lengths[:, None]  1.33 us

profile of v2, /device:TPU:0, one launch (start us, length us, event | category | flops | bytes accessed | tf_op | source)
XLA Modules:
  0.0 53.4 jit_solution(17854202204806726781)
XLA Ops:
  0.0 1.3 %copy.13.route_ref = bf16[16,2]{1,0:T(8,128)(2,1)} copy(bf16[16,2]{0,1:T(2,128)(2,1)} %param.17) | data formatting | bytes 128 | tf_op args[7]
  1.3 1.3 %copy.11.len_ref = s32[16,1]{1,0:T(8,128)} copy(s32[16,1]{0,1:T(1,128)} %bitcast.1) | data formatting | bytes 128 | tf_op jit(solution)/shard_map/broadcast_in_dim | solution.py:313
  2.7 1.3 %copy.12.id_ref = s32[16,2]{1,0:T(8,128)} copy(s32[16,2]{0,1:T(2,128)} %param.16) | data formatting | bytes 256 | tf_op args[6]
  4.0 47.8 %shard_map.100 = bf16[16,3072]{1,0:T(8,128)(2,1)} custom-call(bf16[16,3072]{1,0:T(8,128)(2,1)} %q_ref.1, bf16[16,2,512]{2,1,0:T(2,128)(2,1)} %nkv_ref.1, bf16[16,2,16,512]{3,2,1,0:T(8,128)(2,1)} %cache_ref.1, bf16[16,3072]{1,0:T(8,128)(2,1)} %res_ref.1, bf16[6144]{0:T(1024)(128)(2,1)} %gain_ref.1, s32[16,1]{1,0:T(8,128)} %copy.11.len_ref, ...), custom_call_target="tpu_custom_call" | custom-call | tf_op jit(solution)/shard_map/pallas_call | solution.py:277
  51.8 1.5 %copy.15 = bf16[16,3072]{1,0:T(8,128)(2,1)} copy(bf16[16,3072]{1,0:T(8,128)(2,1)} %shard_map.100) | data formatting | bytes 196608

commit v3 on v2

--- a/solution.py
+++ b/solution.py
@@ -129,7 +129,7 @@
         copy.start()
         sent.append(copy)
 
-    for k in (2, 1, 3):
+    for k in (1, 3, 2):
         start(over_experts(k))
     for i in (0, 1, 3, 2):
         if i:
@@ -236,7 +236,7 @@
         for k in range(1, m):
             total = total + member_arrived(n, k)
         exp_out[n] = total.astype(BF16)
-        for k in (2, 1, 3):
+        for k in (1, 3, 2):
             start(expert_copy(n, k))
 
     def weight(ee):

time: 53.6 us -> 52.1 us (0.972)
  Pallas kernels: 47.8 us -> 46.4 us
    pallas_call x1, Pallas kernels: 47.8 us -> 46.4 us  [local(): pl.pallas_call(functools.partial(kernel, m), out_shape=jax.ShapeDtypeStru...]
where the time goes in v3:
time: 52.1 us; the launch traced here: 51.9 us
  Pallas kernels  46.4 us (89%)
  local copies, waits for them, and re-layouts  5.55 us (11%)
    pallas_call x1, Pallas kernels, local(): pl.pallas_call(functools.partial(kernel, m), out_shape=jax.ShapeDtypeStru...  46.4 us
    unnamed x3, local copies, waits for them, and re-layouts  4.22 us
    broadcast_in_dim x1, local copies, waits for them, and re-layouts, local(): lengths[:, None]  1.33 us

profile of v3, /device:TPU:0, one launch (start us, length us, event | category | flops | bytes accessed | tf_op | source)
XLA Modules:
  0.0 51.9 jit_solution(13141133667802918302)
XLA Ops:
  0.0 1.3 %copy.13.route_ref = bf16[16,2]{1,0:T(8,128)(2,1)} copy(bf16[16,2]{0,1:T(2,128)(2,1)} %param.17) | data formatting | bytes 128 | tf_op args[7]
  1.3 1.3 %copy.11.len_ref = s32[16,1]{1,0:T(8,128)} copy(s32[16,1]{0,1:T(1,128)} %bitcast.1) | data formatting | bytes 128 | tf_op jit(solution)/shard_map/broadcast_in_dim | solution.py:313
  2.7 1.3 %copy.12.id_ref = s32[16,2]{1,0:T(8,128)} copy(s32[16,2]{0,1:T(2,128)} %param.16) | data formatting | bytes 256 | tf_op args[6]
  4.0 46.4 %shard_map.100 = bf16[16,3072]{1,0:T(8,128)(2,1)} custom-call(bf16[16,3072]{1,0:T(8,128)(2,1)} %q_ref.1, bf16[16,2,512]{2,1,0:T(2,128)(2,1)} %nkv_ref.1, bf16[16,2,16,512]{3,2,1,0:T(8,128)(2,1)} %cache_ref.1, bf16[16,3072]{1,0:T(8,128)(2,1)} %res_ref.1, bf16[6144]{0:T(1024)(128)(2,1)} %gain_ref.1, s32[16,1]{1,0:T(8,128)} %copy.11.len_ref, ...), custom_call_target="tpu_custom_call" | custom-call | tf_op jit(solution)/shard_map/pallas_call | solution.py:277
  50.4 1.5 %copy.15 = bf16[16,3072]{1,0:T(8,128)(2,1)} copy(bf16[16,3072]{1,0:T(8,128)(2,1)} %shard_map.100) | data formatting | bytes 196608
